TPU v7x, 128 devices: a whole 4x4x4 slice. The times are simulated.
128 devices in a mesh: row: 16 (over x, y), col: 8 (over z, core).
Axes of the slice: x: 4, y: 4, z: 4, core: 2. Of those that a mesh axis runs over, the one named last changes fastest.
Arguments:
- panel: bfloat16 [49152, 256], P('row', 'col'), as said below
- trailing: bfloat16 [49152, 16384], P('row', 'col'), may hold values from -6 to 6
- tile_list: int32 [352], P('row'), may hold values from 0 to 23, as said below
Outputs:
- triangle: float32 [256, 256], replicated
- top_rows: float32 [16384, 256], P('col')
- updated: bfloat16 [45056, 16384], P('row', 'col')
Inputs may be any that keep to these rules, and one draw needn't show every extreme that they name: `tile_list`: each aligned block of 22 entries (the entries of one index of row) lists distinct tile numbers of that group's 24 tiles in increasing order and always includes tile 24 - 1. `panel`: the active rows of every row group, and all active rows together, have full column rank with a condition number under 100.
All inputs are finite; a program needn't handle non-finite values.
Results may differ from a plain program's by a relative error of at most 0.0065.
Values may be sent and summed in bfloat16 or wider, within the bound.
A program may use at most 128 MiB of HBM per device.

v0:
```python
import jax
import jax.numpy as jnp
from jax import lax
from jax.sharding import PartitionSpec as P

TILE = 128


def sent_to_all(array, axis):
    copies = jnp.broadcast_to(array, (lax.axis_size(axis), *array.shape))
    return lax.all_to_all(copies, axis, split_axis=0, concat_axis=0, tiled=True)


def laid_out(pieces, dim):
    pieces = jnp.moveaxis(pieces, 0, dim)
    shape = pieces.shape
    return pieces.reshape(*shape[:dim], shape[dim] * shape[dim + 1], *shape[dim + 2 :])


def gather_directly(array, axis, dim):
    pieces = sent_to_all(array, axis)
    return laid_out(pieces, dim)


def taken_together(array, axis):
    everything = sent_to_all(array, axis)
    return jnp.sum(everything.astype(jnp.float32), axis=0)


def pick_tiles(whole, tile_list):
    tiled = whole.reshape(-1, TILE, whole.shape[1])
    return jnp.take(tiled, tile_list, axis=0).reshape(-1, whole.shape[1])


def local(panel, trailing, tile_list):
    panel_full = gather_directly(panel, "col", 1)
    act_panel = pick_tiles(panel_full, tile_list)
    act_trail = pick_tiles(trailing, tile_list)
    local_gram = lax.dot_general(
        act_panel, act_panel, (((0,), (0,)), ((), ())), preferred_element_type=jnp.float32
    )
    gram_matrix = taken_together(local_gram.astype(jnp.bfloat16), "row").astype(jnp.float32)
    lower_factor = jnp.linalg.cholesky(gram_matrix)
    triangle = lower_factor.T
    local_cross = lax.dot_general(
        act_trail, act_panel, (((0,), (0,)), ((), ())), preferred_element_type=jnp.float32
    )
    cross_sum = lax.psum(local_cross, "row")
    top_rows = jax.scipy.linalg.solve_triangular(lower_factor, cross_sum.T, lower=True).T
    coeff = jax.scipy.linalg.solve_triangular(
        lower_factor, top_rows.T, lower=True, trans=1
    ).T.astype(jnp.bfloat16)
    product = lax.dot_general(
        act_panel, coeff, (((1,), (1,)), ((), ())), preferred_element_type=jnp.float32
    )
    updated = (act_trail.astype(jnp.float32) - product).astype(jnp.bfloat16)
    return (triangle, top_rows, updated)


def solution(mesh):
    return jax.shard_map(
        local,
        mesh=mesh,
        in_specs=(P("row", "col"), P("row", "col"), P("row")),
        out_specs=(P(), P("col", None), P("row", "col")),
        check_vma=False,
    )
```

profile of v0, /device:TPU:0, one launch (start us, length us, event | category | flops | bytes accessed | tf_op | source)
XLA Modules:
  0.0 185.2 jit_solution(9979115760256562924)
XLA Ops:
  7.2 2.3 %broadcast_in_dim.43 = bf16[8,3072,32]{1,2,0:T(8,128)(2,1)} broadcast(bf16[3072,32]{0,1:T(8,128)(2,1)} %param.3), dimensions={1,2} | broadcast | bytes 1769472 | tf_op jit(solution)/shard_map/broadcast_in_dim | solution.py:10
  9.4 5.4 %all-to-all-start = ((bf16[8,3072,32]{1,2,0:T(8,128)(2,1)}), bf16[8,3072,32]{1,2,0:T(8,128)(2,1)S(1)}, u32[]{:S(2)}, u32[]{:S(2)}) async-start(bf16[8,3072,32]{1,2,0:T(8,128)(2,1)} %broadcast_in_dim.43), calls=%async_computation | async-start | bytes 3145728 | tf_op jit(solution)/shard_map/all_to_all | solution.py:11
  14.9 21.5 %all-to-all-done = bf16[8,3072,32]{1,2,0:T(8,128)(2,1)S(1)} async-done(((bf16[8,3072,32]{1,2,0:T(8,128)(2,1)}), bf16[8,3072,32]{1,2,0:T(8,128)(2,1)S(1)}, u32[]{:S(2)}, u32[]{:S(2)}) %all-to-all-start) | async-done | bytes 1572896 | tf_op jit(solution)/shard_map/all_to_all | solution.py:11
  36.7 1.1 copy.17
  39.4 1.5 broadcast_in_dim.46
  40.9 7.0 %all-to-all-start.1 = ((bf16[16,256,256]{2,1,0:T(8,128)(2,1)}), bf16[16,256,256]{2,1,0:T(8,128)(2,1)S(1)}, u32[]{:S(2)}, u32[]{:S(2)}) async-start(bf16[16,256,256]{2,1,0:T(8,128)(2,1)} %broadcast_in_dim.46), calls=%async_computation.1 | async-start | bytes 4194304 | tf_op jit(solution)/shard_map/all_to_all | solution.py:11
  48.0 10.5 %gather_fusion.1 = bf16[22,128,2048]{2,1,0:T(8,128)(2,1)} fusion(bf16[24,128,2048]{2,1,0:T(8,128)(2,1)} %bitcast.64, s32[1024]{0:T(1024)S(1)} %pad_clamp_fusion), kind=kCustom, calls=%fused_computation.1 | custom fusion | bytes 23068760 | tf_op jit(solution)/shard_map/jit(_take)/gather | solution.py:32
  58.5 8.8 %fusion.4 = f32[256,2048]{1,0:T(8,128)} fusion(bf16[22,128,2048]{2,1,0:T(8,128)(2,1)} %gather_fusion.1, pred[22]{0:T(512)(128)(4,1)S(1)} %compare_and_fusion, bf16[22,128,256]{2,1,0:T(8,128)(2,1)S(1)} %gather_fusion), kind=kOutput, calls=%fused_computation.11 | convolution fusion | flops 2959278080 | bytes 15073302 | tf_op jit(solution)/shard_map/dot_general | solution.py:45
  67.4 2.3 %bitcast_select_fusion.1 = bf16[2816,256]{1,0:T(8,128)(2,1)} fusion(bf16[22,128,256]{2,1,0:T(8,128)(2,1)S(1)} %gather_fusion, pred[2816]{0:T(1024)(128)(4,1)S(1)} %broadcast_bitcast_fusion), kind=kLoop, calls=%fused_computation.16 | loop fusion | flops 720896 | bytes 2886400 | tf_op jit(solution)/shard_map/jit(_take)/select_n | solution.py:32
  69.7 8.2 %all-to-all-done.1 = bf16[16,256,256]{2,1,0:T(8,128)(2,1)S(1)} async-done(((bf16[16,256,256]{2,1,0:T(8,128)(2,1)}), bf16[16,256,256]{2,1,0:T(8,128)(2,1)S(1)}, u32[]{:S(2)}, u32[]{:S(2)}) %all-to-all-start.1) | async-done | bytes 2097184 | tf_op jit(solution)/shard_map/all_to_all | solution.py:11
  78.4 11.7 %cholesky.50 = f32[128,128]{1,0:T(8,128)S(1)} custom-call(f32[128,128]{1,0:T(8,128)S(1)} %cholesky.118), custom_call_target="Cholesky" | custom-call | tf_op jit(solution)/shard_map/jit(cholesky)/cholesky | solution.py:43
  90.2 9.8 %custom-call.18 = f32[1,128,128]{1,2,0:T(8,128)S(1)} custom-call(f32[1,128,128]{2,1,0:T(8,128)S(1)} %get-tuple-element.35), custom_call_target="InvertDiagBlocksLowerTriangular" | custom-call | tf_op jit(solution)/shard_map/jit(cholesky)/cholesky | solution.py:43
  100.5 11.7 %cholesky.105 = f32[128,128]{1,0:T(8,128)S(1)} custom-call(f32[128,128]{1,0:T(8,128)S(1)} %convolution_subtract_fusion.2), custom_call_target="Cholesky" | custom-call | tf_op jit(solution)/shard_map/jit(cholesky)/cholesky | solution.py:43
  115.2 5.2 %while.1 = (s32[]{:T(128)}, f32[256,256]{1,0:T(8,128)S(1)}, s32[2,2]{1,0:T(2,128)S(1)}, f32[2,128,128]{2,1,0:T(8,128)}, s32[]{:T(128)}) while((s32[]{:T(128)}, f32[256,256]{1,0:T(8,128)S(1)}, s32[2,2]{1,0:T(2,128)S(1)}, f32[2,128,128]{2,1,0:T(8,128)}, s32[]{:T(128)}) %tuple.32), condition=%wide.while_cond, body=%wide.while_body.sunk | while | flops 2 | bytes 132205 | solution.py:49
  115.8 2.0 %bitcast_dynamic-update-slice_fusion.2 = f32[2,128,128]{2,1,0:T(8,128)} fusion(f32[2,128,128]{2,1,0:T(8,128)} %get-tuple-element.79, s32[]{:T(128)S(6)} %copy.32, f32[256,256]{1,0:T(8,128)S(1)} %get-tuple-element.82, s32[]{:T(128)} %bitcast.62, s32[]{:T(128)} %bitcast.63), kind=kLoop, calls=%fused_computation.2.clone.1 | loop fusion | bytes 132100 | tf_op jit(solution)/shard_map/jit(_solve_triangular)/triangular_solve
  118.3 2.0 %bitcast_dynamic-update-slice_fusion.2 = f32[2,128,128]{2,1,0:T(8,128)} fusion(f32[2,128,128]{2,1,0:T(8,128)} %get-tuple-element.79, s32[]{:T(128)S(6)} %copy.32, f32[256,256]{1,0:T(8,128)S(1)} %get-tuple-element.82, s32[]{:T(128)} %bitcast.62, s32[]{:T(128)} %bitcast.63), kind=kLoop, calls=%fused_computation.2.clone.1 | loop fusion | bytes 132100 | tf_op jit(solution)/shard_map/jit(_solve_triangular)/triangular_solve
  120.4 20.5 %custom-call.19 = f32[2,128,128]{1,2,0:T(8,128)S(1)} custom-call(f32[2,128,128]{2,1,0:T(8,128)} %get-tuple-element.10), custom_call_target="InvertDiagBlocksLowerTriangular" | custom-call | tf_op jit(solution)/shard_map/jit(_solve_triangular)/triangular_solve | solution.py:49
  140.9 16.8 %all-reduce.3.cloned.1.call-done = f32[256,2048]{1,0:T(8,128)} async-done(((f32[256,2048]{1,0:T(8,128)}), f32[256,2048]{1,0:T(8,128)}) %all-reduce.3.cloned.1.call-update) | async-done | bytes 2097168 | tf_op jit(solution)/shard_map/psum | solution.py:48
  157.7 2.4 %fusion.8 = f32[128,2048]{1,0:T(8,128)S(1)} fusion(f32[256,2048]{1,0:T(8,128)} %all-reduce.3.cloned.1.call-done, f32[2,128,128]{1,2,0:T(8,128)S(1)} %custom-call.19), kind=kOutput, calls=%fused_computation.21 | convolution fusion | flops 402653184 | bytes 2162688 | tf_op jit(solution)/shard_map/jit(_solve_triangular)/triangular_solve | solution.py:49
  162.2 1.8 fusion.27
  164.1 1.1 convolution_subtract_fusion
  165.2 1.8 convolution_convert_fusion
  167.0 1.8 copy.22
  168.9 9.5 %subtract_convert_fusion = bf16[2816,2048]{1,0:T(8,128)(2,1)} fusion(bf16[22,128,2048]{2,1,0:T(8,128)(2,1)} %gather_fusion.1, pred[2816]{0:T(1024)(128)(4,1)S(1)} %broadcast_bitcast_fusion, bf16[2816,256]{1,0:T(8,128)(2,1)S(1)} %copy-done.1, bf16[128,2048]{1,0:T(8,128)(2,1)} %get-tuple-element.38, bf16[128,2048]{1,0:T(8,128)(2,1)} %convolution_convert_fusion), kind=kOutput, calls=%fused_computation.4 | convolution fusion | flops 2977955840 | bytes 25561856 | tf_op jit(solution)/shard_map/dot_general | solution.py:53
  (37 shorter events, 8.0 us)
Async XLA Ops:
  7.2 7.7 %copy-start.2 = (s32[22]{0:T(128)S(1)}, s32[22]{0:T(128)}, u32[]{:S(2)}) copy-start(s32[22]{0:T(128)} %param.5) | copy-start | bytes 268
  9.4 27.0 %all-to-all-start = ((bf16[8,3072,32]{1,2,0:T(8,128)(2,1)}), bf16[8,3072,32]{1,2,0:T(8,128)(2,1)S(1)}, u32[]{:S(2)}, u32[]{:S(2)}) async-start(bf16[8,3072,32]{1,2,0:T(8,128)(2,1)} %broadcast_in_dim.43), calls=%async_computation | async-start | bytes 3145728 | tf_op jit(solution)/shard_map/all_to_all | solution.py:11
  40.9 37.0 %all-to-all-start.1 = ((bf16[16,256,256]{2,1,0:T(8,128)(2,1)}), bf16[16,256,256]{2,1,0:T(8,128)(2,1)S(1)}, u32[]{:S(2)}, u32[]{:S(2)}) async-start(bf16[16,256,256]{2,1,0:T(8,128)(2,1)} %broadcast_in_dim.46), calls=%async_computation.1 | async-start | bytes 4194304 | tf_op jit(solution)/shard_map/all_to_all | solution.py:11
  48.0 109.7 %all-reduce.3.cloned.1.call-start = ((), (), s32[]{:S(2)}) async-start(), calls=%async_computation.2 | async-start | bytes 4194304 | tf_op jit(solution)/shard_map/psum | solution.py:48
  157.7 2.4 %copy-start = (f32[256,2048]{1,0:T(8,128)S(1)}, f32[256,2048]{1,0:T(8,128)}, u32[]{:S(2)}) copy-start(f32[256,2048]{1,0:T(8,128)} %all-reduce.3.cloned.1.call-done) | copy-start | bytes 6291460
  167.0 1.8 copy-start.1
Sparse Core Ops, SparseCore 0:
  67.5 90.1 all-reduce.2
where the time goes:
time: 186 us; the launch traced here: 185 us
  other arithmetic  57.3 us (31%)
  waiting for transfers between devices  46.5 us (25%)
  matrix products  28.8 us (15%)
  local copies, waits for them, and re-layouts  24.5 us (13%)
  between operations  15.5 us (8%)
  starting transfers between devices  12.5 us (7%)
    another operation x6, other arithmetic, local(): lower_factor = jnp.linalg.cholesky(gram_matrix)  34 us
    all_to_all x2, waiting for transfers between devices, sent_to_all(): return lax.all_to_all(copies, axis, split_axis=0, concat_axis=0, tiled=True)  29.7 us
    another operation x3, other arithmetic, local(): jax.scipy.linalg.solve_triangular(lower_factor, cross_sum.T, lower=True)  20.5 us
    psum x1, waiting for transfers between devices, local(): cross_sum = lax.psum(local_cross, 'row')  16.8 us
    all_to_all x2, starting transfers between devices, sent_to_all(): return lax.all_to_all(copies, axis, split_axis=0, concat_axis=0, tiled=True)  12.4 us
    gather x2, local copies, waits for them, and re-layouts, pick_tiles(): return jnp.take(tiled, tile_list, axis=0).reshape(-1, whole.shape[1])  11.1 us
    dot_general x1, matrix products, local(): lax.dot_general(act_panel, coeff, (((1,), (1,)), ((), ())), preferred_ele...  9.49 us
    dot_general x1, matrix products, local(): lax.dot_general(act_trail, act_panel, (((0,), (0,)), ((), ())), preferred...  8.84 us
  transfers between devices with their start and end apart: 3, of which 3 were waited for; matrix products, arithmetic and copies ran while one was open for 45% of the time, Pallas kernels for 0%

commit v1 on v0

--- a/solution.py
+++ b/solution.py
@@ -45,7 +45,8 @@
     local_cross = lax.dot_general(
         act_trail, act_panel, (((0,), (0,)), ((), ())), preferred_element_type=jnp.float32
     )
-    cross_sum = lax.psum(local_cross, "row")
+    parts = lax.all_gather(local_cross, "row")
+    cross_sum = jnp.sum(parts, axis=0)
     top_rows = jax.scipy.linalg.solve_triangular(lower_factor, cross_sum.T, lower=True).T
     coeff = jax.scipy.linalg.solve_triangular(
         lower_factor, top_rows.T, lower=True, trans=1

time: 186 us -> 305 us (1.64)
  waiting for transfers between devices: 46.5 us -> 150 us
  other arithmetic: 57.3 us -> 69.4 us
    all_gather x0 -> x1, waiting for transfers between devices: none -> 97 us  [local(): parts = lax.all_gather(local_cross, 'row')]
    all_to_all x2, waiting for transfers between devices: 29.7 us -> 53.2 us  [sent_to_all(): return lax.all_to_all(copies, axis, split_axis=0, concat_axis=0, tiled=True)]
    psum x1 -> x0, waiting for transfers between devices: 16.8 us -> none  [local(): cross_sum = lax.psum(local_cross, 'row')]
    reduce_sum x0 -> x1, other arithmetic: none -> 12.1 us  [local(): cross_sum = jnp.sum(parts, axis=0)]
  transfers between devices with their start and end apart: 3 -> 3, of which waited for: 3 -> 3; matrix products, arithmetic and copies ran while one was open for 45% -> 25% of each run, Pallas kernels for 0% -> 0%
where the time goes in v1:
time: 305 us; the launch traced here: 304 us
  waiting for transfers between devices  150 us (49%)
  other arithmetic  69.4 us (23%)
  matrix products  30.1 us (10%)
  local copies, waits for them, and re-layouts  26.3 us (9%)
  between operations  15.6 us (5%)
  starting transfers between devices  12.5 us (4%)
    all_gather x1, waiting for transfers between devices, local(): parts = lax.all_gather(local_cross, 'row')  97 us
    all_to_all x2, waiting for transfers between devices, sent_to_all(): return lax.all_to_all(copies, axis, split_axis=0, concat_axis=0, tiled=True)  53.2 us
    another operation x6, other arithmetic, local(): lower_factor = jnp.linalg.cholesky(gram_matrix)  33.9 us
    another operation x3, other arithmetic, local(): jax.scipy.linalg.solve_triangular(lower_factor, cross_sum.T, lower=True)  20.5 us
    all_to_all x2, starting transfers between devices, sent_to_all(): return lax.all_to_all(copies, axis, split_axis=0, concat_axis=0, tiled=True)  12.4 us
    reduce_sum x1, other arithmetic, local(): cross_sum = jnp.sum(parts, axis=0)  12.1 us
    gather x2, local copies, waits for them, and re-layouts, pick_tiles(): return jnp.take(tiled, tile_list, axis=0).reshape(-1, whole.shape[1])  11 us
    dot_general x1, matrix products, local(): lax.dot_general(act_trail, act_panel, (((0,), (0,)), ((), ())), preferred...  9.38 us
  transfers between devices with their start and end apart: 3, of which 3 were waited for; matrix products, arithmetic and copies ran while one was open for 25% of the time, Pallas kernels for 0%

profile of v1, /device:TPU:0, one launch (start us, length us, event | category | flops | bytes accessed | tf_op | source)
XLA Modules:
  0.0 304.0 jit_solution(12988428908643971038)
XLA Ops:
  7.2 2.3 broadcast_in_dim.43
  9.4 5.4 %all-to-all-start = ((bf16[8,3072,32]{1,2,0:T(8,128)(2,1)}), bf16[8,3072,32]{1,2,0:T(8,128)(2,1)S(1)}, u32[]{:S(2)}, u32[]{:S(2)}) async-start(bf16[8,3072,32]{1,2,0:T(8,128)(2,1)} %broadcast_in_dim.43), calls=%async_computation | async-start | bytes 3145728 | tf_op jit(solution)/shard_map/all_to_all | solution.py:11
  14.9 10.4 %gather_fusion.1 = bf16[22,128,2048]{2,1,0:T(8,128)(2,1)} fusion(bf16[24,128,2048]{2,1,0:T(8,128)(2,1)} %bitcast.67, s32[1024]{0:T(1024)S(1)} %pad_clamp_fusion), kind=kCustom, calls=%fused_computation.1 | custom fusion | bytes 23068760 | tf_op jit(solution)/shard_map/jit(_take)/gather | solution.py:32
  25.3 11.1 %all-to-all-done = bf16[8,3072,32]{1,2,0:T(8,128)(2,1)S(1)} async-done(((bf16[8,3072,32]{1,2,0:T(8,128)(2,1)}), bf16[8,3072,32]{1,2,0:T(8,128)(2,1)S(1)}, u32[]{:S(2)}, u32[]{:S(2)}) %all-to-all-start) | async-done | bytes 1572896 | tf_op jit(solution)/shard_map/all_to_all | solution.py:11
  38.5 9.4 %fusion.4 = f32[2048,256]{1,0:T(8,128)} fusion(bf16[22,128,2048]{2,1,0:T(8,128)(2,1)} %gather_fusion.1, pred[22]{0:T(512)(128)(4,1)S(1)} %compare_and_fusion, bf16[22,128,256]{2,1,0:T(8,128)(2,1)S(1)} %gather_fusion), kind=kOutput, calls=%fused_computation.11 | convolution fusion | flops 2959278080 | bytes 15073302 | tf_op jit(solution)/shard_map/dot_general | solution.py:45
  48.8 1.5 broadcast_in_dim.46
  50.3 7.0 %all-to-all-start.1 = ((bf16[16,256,256]{2,1,0:T(8,128)(2,1)}), bf16[16,256,256]{2,1,0:T(8,128)(2,1)S(1)}, u32[]{:S(2)}, u32[]{:S(2)}) async-start(bf16[16,256,256]{2,1,0:T(8,128)(2,1)} %broadcast_in_dim.46), calls=%async_computation.1 | async-start | bytes 4194304 | tf_op jit(solution)/shard_map/all_to_all | solution.py:11
  57.5 2.3 bitcast_select_fusion.1
  59.8 42.1 %all-to-all-done.1 = bf16[16,256,256]{2,1,0:T(8,128)(2,1)S(1)} async-done(((bf16[16,256,256]{2,1,0:T(8,128)(2,1)}), bf16[16,256,256]{2,1,0:T(8,128)(2,1)S(1)}, u32[]{:S(2)}, u32[]{:S(2)}) %all-to-all-start.1) | async-done | bytes 2097184 | tf_op jit(solution)/shard_map/all_to_all | solution.py:11
  102.4 11.7 %cholesky.50 = f32[128,128]{1,0:T(8,128)S(1)} custom-call(f32[128,128]{1,0:T(8,128)S(1)} %cholesky.118), custom_call_target="Cholesky" | custom-call | tf_op jit(solution)/shard_map/jit(cholesky)/cholesky | solution.py:43
  114.1 9.8 %custom-call.18 = f32[1,128,128]{1,2,0:T(8,128)S(1)} custom-call(f32[1,128,128]{2,1,0:T(8,128)S(1)} %get-tuple-element.41), custom_call_target="InvertDiagBlocksLowerTriangular" | custom-call | tf_op jit(solution)/shard_map/jit(cholesky)/cholesky | solution.py:43
  124.4 11.7 %cholesky.105 = f32[128,128]{1,0:T(8,128)S(1)} custom-call(f32[128,128]{1,0:T(8,128)S(1)} %convolution_subtract_fusion.2), custom_call_target="Cholesky" | custom-call | tf_op jit(solution)/shard_map/jit(cholesky)/cholesky | solution.py:43
  139.1 5.3 %while.1 = (s32[]{:T(128)}, f32[256,256]{1,0:T(8,128)S(1)}, s32[2,2]{1,0:T(2,128)S(1)}, f32[2,128,128]{2,1,0:T(8,128)}, s32[]{:T(128)}) while((s32[]{:T(128)}, f32[256,256]{1,0:T(8,128)S(1)}, s32[2,2]{1,0:T(2,128)S(1)}, f32[2,128,128]{2,1,0:T(8,128)}, s32[]{:T(128)}) %tuple.34), condition=%wide.while_cond, body=%wide.while_body.sunk | while | flops 2 | bytes 132205 | solution.py:50
  139.7 2.0 bitcast_dynamic-update-slice_fusion.2
  142.3 2.0 bitcast_dynamic-update-slice_fusion.2
  144.4 20.5 %custom-call.19 = f32[2,128,128]{1,2,0:T(8,128)S(1)} custom-call(f32[2,128,128]{2,1,0:T(8,128)} %get-tuple-element.10), custom_call_target="InvertDiagBlocksLowerTriangular" | custom-call | tf_op jit(solution)/shard_map/jit(_solve_triangular)/triangular_solve | solution.py:50
  164.9 97.0 %all-gather.3.cloned.1.call-done = f32[32768,256]{1,0:T(8,128)} async-done(((f32[2048,256]{1,0:T(8,128)}), f32[32768,256]{1,0:T(8,128)}) %all-gather.3.cloned.1.call-update) | async-done | bytes 33554448 | tf_op jit(solution)/shard_map/all_gather | solution.py:48
  261.9 12.1 %reduce_sum.19 = f32[2048,256]{1,0:T(8,128)S(1)} reduce(f32[16,2048,256]{2,1,0:T(8,128)} %bitcast.66, f32[]{:T(128)} %constant.112.clone.1), dimensions={0}, to_apply=%region_5.6 | reduce | flops 7864320 | bytes 35651588 | tf_op jit(solution)/shard_map/reduce_sum | solution.py:49
  273.9 1.8 copy.36
  275.7 2.4 fusion.8
  280.4 2.1 fusion.27
  282.6 1.8 copy.38
  284.4 2.4 convolution_subtract_fusion
  287.8 9.3 %subtract_convert_fusion = bf16[2816,2048]{1,0:T(8,128)(2,1)} fusion(bf16[22,128,2048]{2,1,0:T(8,128)(2,1)} %gather_fusion.1, pred[2816]{0:T(1024)(128)(4,1)S(1)} %broadcast_bitcast_fusion, bf16[2816,256]{1,0:T(8,128)(2,1)S(1)} %copy-done.1, bf16[128,2048]{1,0:T(8,128)(2,1)S(1)} %copy-done.2, bf16[128,2048]{1,0:T(8,128)(2,1)S(1)} %convolution_convert_fusion), kind=kOutput, calls=%fused_computation.4 | convolution fusion | flops 2977955840 | bytes 25561856 | tf_op jit(solution)/shard_map/dot_general | solution.py:54
  (41 shorter events, 10.2 us)
Async XLA Ops:
  7.2 7.7 %copy-start.3 = (s32[22]{0:T(128)S(1)}, s32[22]{0:T(128)}, u32[]{:S(2)}) copy-start(s32[22]{0:T(128)} %param.5) | copy-start | bytes 268
  9.4 27.0 %all-to-all-start = ((bf16[8,3072,32]{1,2,0:T(8,128)(2,1)}), bf16[8,3072,32]{1,2,0:T(8,128)(2,1)S(1)}, u32[]{:S(2)}, u32[]{:S(2)}) async-start(bf16[8,3072,32]{1,2,0:T(8,128)(2,1)} %broadcast_in_dim.43), calls=%async_computation | async-start | bytes 3145728 | tf_op jit(solution)/shard_map/all_to_all | solution.py:11
  14.8 247.0 %all-gather.3.cloned.1.call-start = ((), (), s32[]{:S(2)}) async-start(), calls=%async_computation.2 | async-start | bytes 35651584 | tf_op jit(solution)/shard_map/all_gather | solution.py:48
  50.3 51.5 %all-to-all-start.1 = ((bf16[16,256,256]{2,1,0:T(8,128)(2,1)}), bf16[16,256,256]{2,1,0:T(8,128)(2,1)S(1)}, u32[]{:S(2)}, u32[]{:S(2)}) async-start(bf16[16,256,256]{2,1,0:T(8,128)(2,1)} %broadcast_in_dim.46), calls=%async_computation.1 | async-start | bytes 4194304 | tf_op jit(solution)/shard_map/all_to_all | solution.py:11
  275.7 2.4 copy-start
  284.4 3.4 %copy-start.1 = (bf16[2816,256]{1,0:T(8,128)(2,1)S(1)}, bf16[2816,256]{1,0:T(8,128)(2,1)}, u32[]{:S(2)}) copy-start(bf16[2816,256]{1,0:T(8,128)(2,1)} %bitcast_select_fusion.1) | copy-start | bytes 4325380
  284.4 3.4 %copy-start.2 = (bf16[128,2048]{1,0:T(8,128)(2,1)S(1)}, bf16[128,2048]{1,0:T(8,128)(2,1)}, u32[]{:S(2)}) copy-start(bf16[128,2048]{1,0:T(8,128)(2,1)} %get-tuple-element.44) | copy-start | bytes 1572868
Sparse Core Ops, SparseCore 0:
  48.0 213.7 all-gather.2
